TPU v7x, 32 devices: a whole 2x2x4 slice. The times are simulated.
32 devices in a mesh: branch: 4 (over y, x), row: 8 (over z, core).
Axes of the slice: x: 2, y: 2, z: 4, core: 2. Of those that a mesh axis runs over, the one named last changes fastest.
Arguments:
- root_cov: bfloat16 [2304, 2304], P('row', 'branch')
- diag_factor: float32 [4, 3, 576, 576], P('branch')
- panel_factor: float32 [4, 3, 2304, 576], P('branch', None, 'row'), may hold values from -0.009765625 to 0.009765625
- chain_factor: float32 [4, 2, 576, 576], P('branch'), may hold values from -0.25 to 0.25
- panel_tiles: int32 [4, 3], P('branch'), may hold values from 0 to 3, as said below
Outputs:
- panel_cov: float32 [4, 3, 2304, 576], P('branch', None, 'row')
- block_cov: float32 [4, 5, 576, 576], P('branch')
Inputs may be any that keep to these rules, and one draw needn't show every extreme that they name: `panel_tiles`: the entries of a row are distinct; the first 2 and the first 1 entries of a row are the level-two and level-three patterns.
All inputs are finite; a program needn't handle non-finite values.
Results may differ from a plain program's by a relative error of at most 0.0029.
Values may be sent and summed in bfloat16 or wider, within the bound.
A program may use at most 192 MiB of HBM per device.

v0:
```python
import functools
import jax
import jax.numpy as jnp
from jax import lax
from jax.experimental import pallas as pl
from jax.experimental.pallas import tpu as pltpu
from jax.sharding import PartitionSpec as P

BF = jnp.bfloat16
F32 = jnp.float32
MESH = pl.DeviceIdType.MESH


def product(left_mat, right_mat):
    return jnp.dot(left_mat, right_mat, precision=lax.Precision.HIGH, preferred_element_type=F32)


def split(x):
    hi = x.astype(BF)
    return hi, (x - hi.astype(F32)).astype(BF)


def mm(a, b):
    return jnp.dot(a, b, preferred_element_type=F32)


def dot3(a, b):
    a_hi, a_lo = a
    b_hi, b_lo = b
    return mm(a_hi, b_hi) + (mm(a_lo, b_hi) + mm(a_hi, b_lo))


def inverse_kernel(size, window, l_ref, out_ref):
    count = size // window
    row = lax.broadcasted_iota(jnp.int32, (window, window), 0)
    col = lax.broadcasted_iota(jnp.int32, (window, window), 1)
    eye = row == col
    diagonals = []
    for w in range(count):
        at = slice(w * window, (w + 1) * window)
        block = l_ref[0, 0, at, at]
        kept = jnp.where(eye, block, 0.0)
        down = 1.0 / jnp.sum(kept, axis=1, keepdims=True)
        across = 1.0 / jnp.sum(kept, axis=0, keepdims=True)
        diagonals.append((block * down, across))
    found = []
    for scaled, across in diagonals:
        x = jnp.where(eye, 1.0, 0.0)
        x = x - jnp.where((row // 2 == col // 2) & (row > col), scaled, 0.0)
        found.append(x)
    k = 2
    while k < window:
        pair = (row // (2 * k) == col // (2 * k)) & (row // k > col // k)
        for w in range(count):
            x = found[w]
            parts = split(x)
            right = dot3(split(jnp.where(pair, diagonals[w][0], 0.0)), parts)
            found[w] = x - dot3(parts, split(right))
        k *= 2
    found = [x * diagonals[w][1] for w, x in enumerate(found)]
    done = {}
    for w in range(count):
        done[w, w] = split(found[w])
        out_ref[0, w * window:(w + 1) * window, w * window:(w + 1) * window] = found[w]
    for gap in range(1, count):
        for c in range(count - gap):
            r = c + gap
            total = None
            for m in range(c, r):
                below = split(l_ref[0, 0, r * window:(r + 1) * window, m * window:(m + 1) * window])
                term = dot3(below, done[m, c])
                total = term if total is None else total + term
            value = -dot3(done[r, r], split(total))
            done[r, c] = split(value)
            out_ref[0, r * window:(r + 1) * window, c * window:(c + 1) * window] = value
            out_ref[0, c * window:(c + 1) * window, r * window:(r + 1) * window] = jnp.zeros(
                (window, window), F32
            )


def inverses(diag_factor):
    levels, size = diag_factor.shape[1], diag_factor.shape[-1]
    return pl.pallas_call(
        functools.partial(inverse_kernel, size, size // 3),
        grid=(levels,),
        in_specs=[pl.BlockSpec((1, 1, size, size), lambda i: (0, i, 0, 0))],
        out_specs=pl.BlockSpec((1, size, size), lambda i: (i, 0, 0)),
        out_shape=jax.ShapeDtypeStruct((levels, size, size), F32),
        compiler_params=pltpu.CompilerParams(vmem_limit_bytes=48 * 2**20),
        name="inverses",
    )(diag_factor)


def sum_kernel(x_ref, out_ref, pair, send, landed, right_got, left_got, right_sib, left_sib, final,
               final_sib, pair_s, pair_r, rs_s, rs_r, right_s, right_r, left_s, left_r, sib_s, sib_r):
    me = lax.axis_index("row")
    z = me // 2
    core = me % 2
    sibling = 2 * z + 1 - core

    def at_chip(chip):
        return {"row": 2 * chip + core}

    barrier = pltpu.get_barrier_semaphore()
    pl.semaphore_signal(barrier, inc=1, device_id={"row": sibling}, device_id_type=MESH)
    for k in (1, 2, 3):
        pl.semaphore_signal(
            barrier, inc=1, device_id=at_chip((z + k) % 4), device_id_type=MESH
        )
    pl.semaphore_wait(barrier, 4)

    def copy(src, dst, send_sem, recv_sem, target):
        return pltpu.make_async_remote_copy(
            src_ref=src, dst_ref=dst, send_sem=send_sem, recv_sem=recv_sem,
            device_id=target, device_id_type=MESH,
        )

    to_pair = {}
    for k in (2, 1, 3, 0):
        to_pair[k] = copy(
            x_ref.at[1 - core, (z + k) % 4], pair.at[k], pair_s.at[k], pair_r.at[k],
            {"row": sibling},
        )
        to_pair[k].start()
    scatter = {}
    for k in (2, 1, 3):
        to_pair[k].wait_recv()
        send[k - 1] = (x_ref[core, (z + k) % 4] + pair[k]).astype(BF)
        scatter[k] = copy(
            send.at[k - 1], landed.at[k - 1], rs_s.at[k - 1], rs_r.at[k - 1],
            at_chip((z + k) % 4),
        )
        scatter[k].start()
    to_pair[0].wait_recv()
    pair[0] = pair[0] + x_ref[core, z]
    for k in (1, 3, 2):
        scatter[k].wait_recv()
        pair[0] = pair[0] + landed[k - 1].astype(F32)
    final[...] = pair[0].astype(BF)

    rights, lefts, sibs = {}, {}, {}
    sibs[0] = copy(final, final_sib, sib_s.at[0], sib_r.at[0], {"row": sibling})
    for s in (1, 2, 3):
        rights[s] = copy(
            final if s == 1 else right_got.at[s - 2], right_got.at[s - 1],
            right_s.at[s - 1], right_r.at[s - 1], at_chip(jnp.minimum(z + 1, 3)),
        )
        lefts[s] = copy(
            final if s == 1 else left_got.at[s - 2], left_got.at[s - 1],
            left_s.at[s - 1], left_r.at[s - 1], at_chip(jnp.maximum(z - 1, 0)),
        )
        sibs[s] = copy(
            right_got.at[s - 1], right_sib.at[s - 1], sib_s.at[s], sib_r.at[s], {"row": sibling}
        )
        sibs[-s] = copy(
            left_got.at[s - 1], left_sib.at[s - 1], sib_s.at[3 + s], sib_r.at[3 + s],
            {"row": sibling},
        )

    def goes_right(s):
        return (z < 3) & (z >= s - 1)

    def goes_left(s):
        return (z > 0) & (z + s <= 4)

    pl.when(goes_right(1))(rights[1].start)
    pl.when(goes_left(1))(lefts[1].start)
    sibs[0].start()
    out_ref[core, z] = final[...].astype(F32)
    for s in (1, 2, 3):
        @pl.when(z >= s)
        def _():
            rights[s].wait_recv()
            sibs[s].start()

        if s < 3:
            pl.when(goes_right(s + 1))(rights[s + 1].start)

        @pl.when(z + s <= 3)
        def _():
            lefts[s].wait_recv()
            sibs[-s].start()

        if s < 3:
            pl.when(goes_left(s + 1))(lefts[s + 1].start)

        @pl.when(z >= s)
        def _():
            out_ref[core, z - s] = right_got[s - 1].astype(F32)

        @pl.when(z + s <= 3)
        def _():
            out_ref[core, z + s] = left_got[s - 1].astype(F32)

    sibs[0].wait_recv()
    out_ref[1 - core, z] = final_sib[...].astype(F32)
    for s in (1, 2, 3):
        @pl.when(z >= s)
        def _():
            sibs[s].wait_recv()
            out_ref[1 - core, z - s] = right_sib[s - 1].astype(F32)

        @pl.when(z + s <= 3)
        def _():
            sibs[-s].wait_recv()
            out_ref[1 - core, z + s] = left_sib[s - 1].astype(F32)

    for k in (0, 1, 2, 3):
        to_pair[k].wait_send()
        if k:
            scatter[k].wait_send()
    sibs[0].wait_send()
    for s in (1, 2, 3):
        pl.when(goes_right(s))(rights[s].wait_send)
        pl.when(goes_left(s))(lefts[s].wait_send)
        pl.when(z >= s)(sibs[s].wait_send)
        pl.when(z + s <= 3)(sibs[-s].wait_send)


def line_sum(x, total):
    rows, columns = x.shape[0] // 8, x.shape[1]
    dma = pltpu.SemaphoreType.DMA
    whole = pl.BlockSpec(memory_space=pltpu.VMEM)
    out = pl.pallas_call(
        sum_kernel,
        out_shape=jax.ShapeDtypeStruct((2, 4, rows, columns), F32),
        in_specs=[whole],
        out_specs=whole,
        scratch_shapes=[
            pltpu.VMEM((4, rows, columns), F32),
            *[pltpu.VMEM((3, rows, columns), BF) for _ in range(6)],
            pltpu.VMEM((rows, columns), BF),
            pltpu.VMEM((rows, columns), BF),
            dma((4,)), dma((4,)),
            *[dma((3,)) for _ in range(6)],
            dma((7,)), dma((7,)),
        ],
        compiler_params=pltpu.CompilerParams(
            collective_id=0, has_side_effects=True, vmem_limit_bytes=48 * 2**20
        ),
        name="line_sum",
    )(x.reshape(2, 4, rows, columns))
    return out.reshape(8 * rows, columns)[:total]


def gather_kernel(x_ref, out_ref, right_s, right_r, left_s, left_r, sib_s, sib_r, own_s):
    me = lax.axis_index("row")
    z = me // 2
    core = me % 2
    sibling = 2 * z + 1 - core
    right = 2 * jnp.minimum(z + 1, 3) + core
    left = 2 * jnp.maximum(z - 1, 0) + core
    barrier = pltpu.get_barrier_semaphore()
    pl.semaphore_signal(barrier, inc=1, device_id={"row": sibling}, device_id_type=MESH)
    for k in (1, 2, 3):
        pl.semaphore_signal(
            barrier, inc=1, device_id={"row": 2 * ((z + k) % 4) + core}, device_id_type=MESH
        )
    pl.semaphore_wait(barrier, 4)

    def moved(source, part, send_sem, recv_sem, target, first):
        return pltpu.make_async_remote_copy(
            src_ref=x_ref.at[part] if first else out_ref.at[source, part],
            dst_ref=out_ref.at[source, part], send_sem=send_sem, recv_sem=recv_sem,
            device_id={"row": target}, device_id_type=MESH,
        )

    steps = [(s, p) for s in (1, 2, 3) for p in (0, 1)]
    rights, lefts, sib_right, sib_left, own = {}, {}, {}, {}, {}
    for p in (0, 1):
        own[p] = moved(me, p, sib_s.at[0, p], sib_r.at[0, p], sibling, True)
    for s, p in steps:
        from_left = 2 * jnp.maximum(z - s, 0) + core
        from_right = 2 * jnp.minimum(z + s, 3) + core
        rights[s, p] = moved(
            2 * jnp.maximum(z - s + 1, 0) + core, p, right_s.at[s - 1, p], right_r.at[s - 1, p],
            right, s == 1,
        )
        lefts[s, p] = moved(
            2 * jnp.minimum(z + s - 1, 3) + core, p, left_s.at[s - 1, p], left_r.at[s - 1, p],
            left, s == 1,
        )
        sib_right[s, p] = moved(from_left, p, sib_s.at[s, p], sib_r.at[s, p], sibling, False)
        sib_left[s, p] = moved(
            from_right, p, sib_s.at[3 + s, p], sib_r.at[3 + s, p], sibling, False
        )

    def goes_right(s):
        return (z < 3) & (z >= s - 1)

    def goes_left(s):
        return (z > 0) & (z + s <= 4)

    for p in (0, 1):
        pl.when(goes_right(1))(rights[1, p].start)
        pl.when(goes_left(1))(lefts[1, p].start)
    for p in (0, 1):
        own[p].start()
    keep = pltpu.make_async_copy(x_ref, out_ref.at[me], own_s)
    keep.start()
    for s, p in steps:
        @pl.when(z >= s)
        def _():
            rights[s, p].wait_recv()
            sib_right[s, p].start()

        if s < 3:
            pl.when(goes_right(s + 1))(rights[s + 1, p].start)

        @pl.when(z + s <= 3)
        def _():
            lefts[s, p].wait_recv()
            sib_left[s, p].start()

        if s < 3:
            pl.when(goes_left(s + 1))(lefts[s + 1, p].start)
    keep.wait()
    for p in (0, 1):
        own[p].wait()
    for s, p in steps:
        pl.when(goes_right(s))(rights[s, p].wait_send)
        pl.when(goes_left(s))(lefts[s, p].wait_send)
        pl.when(z >= s)(sib_right[s, p].wait)
        pl.when(z + s <= 3)(sib_left[s, p].wait)


def line_gather(x):
    dma = pltpu.SemaphoreType.DMA
    whole = pl.BlockSpec(memory_space=pltpu.VMEM)
    return pl.pallas_call(
        gather_kernel,
        out_shape=jax.ShapeDtypeStruct((8, *x.shape), x.dtype),
        in_specs=[whole],
        out_specs=whole,
        scratch_shapes=[*[dma((3, 2)) for _ in range(4)], dma((7, 2)), dma((7, 2)), dma(())],
        compiler_params=pltpu.CompilerParams(
            collective_id=1, has_side_effects=True, vmem_limit_bytes=32 * 2**20
        ),
        name="line_gather",
    )(x)


def dot3t(a, b):
    def one(p, q):
        return lax.dot_general(p, q, (((0,), (0,)), ((), ())), preferred_element_type=F32)

    return one(a[0], b[0]) + (one(a[1], b[0]) + one(a[0], b[1]))


def partial_kernel(size, keep_ref, root_ref, all_ref, pair_ref, scaled_ref, mine_ref, chain_ref,
                   panel_ref, part_ref):
    tile = lax.axis_index("row") // 2
    panel = block = None
    for i in range(3):
        if i < 2:
            projected = None
            for b in range(4):
                term = mm(root_ref[b], all_ref[2 * b:2 * b + 2, i].reshape(size, size))
                projected = term if projected is None else projected + term
        else:
            projected = mm(root_ref[tile], pair_ref[...])
        scaled = split(scaled_ref[i])
        mine = split(mine_ref[i])
        if i:
            chain = split(chain_ref[i - 1])
            projected = projected + dot3(panel, chain)
            cross = -(dot3t(panel, scaled) + dot3(block, chain))
            part_ref[(2 + i) * size:(3 + i) * size] = cross
        kept = jnp.where(keep_ref[i] > 0, -projected, 0.0)
        panel_ref[0, i] = kept
        panel = split(kept)
        value = dot3t(mine, mine) - dot3t(scaled, panel)
        if i:
            value = value - dot3t(chain, split(cross))
        part_ref[i * size:(i + 1) * size] = value
        block = split(value)
    rest = part_ref.shape[0] - 5 * size
    part_ref[5 * size:] = jnp.zeros((rest, size), F32)


def partials(keep, root, everyone, pair, scaled, mine, chain):
    size = scaled.shape[-1]
    rows = -(-5 * size // 128) * 128
    whole = pl.BlockSpec(memory_space=pltpu.VMEM)
    return pl.pallas_call(
        functools.partial(partial_kernel, size),
        out_shape=(
            jax.ShapeDtypeStruct((1, *scaled.shape), F32),
            jax.ShapeDtypeStruct((rows, size), F32),
        ),
        in_specs=[pl.BlockSpec(memory_space=pltpu.SMEM)] + [whole] * 6,
        out_specs=(whole, whole),
        compiler_params=pltpu.CompilerParams(vmem_limit_bytes=52 * 2**20),
        name="partials",
    )(keep, root, everyone, pair, scaled, mine, chain)


def on_device(root_cov, diag_factor, panel_factor, chain_factor, panel_tiles):
    node_width = diag_factor.shape[-1]
    rows_here = panel_factor.shape[2]
    per_tile = node_width // rows_here
    row_count = lax.axis_size("row")
    tile_total = row_count // per_tile
    counts = (3 * tile_total // 4, tile_total // 2, tile_total // 4)
    small = row_count == 8 and tile_total == 4 and root_cov.shape[1] == node_width
    if small:
        root_rows = lax.all_gather(root_cov, "branch")
    else:
        root_rows = lax.all_gather(root_cov, "branch", axis=1, tiled=True)
    me = lax.axis_index("row")
    my_tile = me // per_tile
    inverse_all = inverses(diag_factor)
    share = -(-node_width // row_count // 8) * 8
    padded = jnp.pad(inverse_all, ((0, 0), (0, share * row_count - node_width), (0, 0)))
    mine = lax.dynamic_slice_in_dim(padded, me * share, share, axis=1)
    chosen = [jnp.any(panel_tiles[0, : counts[i]] == my_tile) for i in range(3)]
    scaled = [
        jnp.where(chosen[i], product(panel_factor[0, i], inverse_all[i]), 0.0) for i in range(3)
    ]
    if small:
        rounded = [x.astype(BF) for x in scaled]
        theirs = lax.ppermute(rounded[2], "row", [(d, d ^ 1) for d in range(row_count)])
        pair = jnp.where(
            me % 2 == 0,
            jnp.concatenate([rounded[2], theirs]),
            jnp.concatenate([theirs, rounded[2]]),
        )
        everyone = line_gather(jnp.stack(rounded[:2]))
        chain_all = jnp.stack([product(chain_factor[0, i - 1], inverse_all[i]) for i in (1, 2)])
        panel_out, parts = partials(
            jnp.stack(chosen).astype(jnp.int32), root_rows, everyone, pair, jnp.stack(scaled),
            mine, chain_all,
        )
        total = line_sum(parts, 5 * node_width)
        return (panel_out, total.reshape(1, 5, node_width, node_width))
    panels = []
    blocks = []
    crosses = []
    for i in range(3):
        rounded = scaled[i].astype(BF)
        gathered = jnp.dot(
            root_rows,
            lax.all_gather(rounded, "row", axis=0, tiled=True),
            preferred_element_type=F32,
        )
        left = jnp.concatenate([mine[i], scaled[i]], axis=0)
        if i == 0:
            panel = -jnp.where(chosen[i], gathered, 0.0)
            block = product(left.T, jnp.concatenate([mine[i], -panel], axis=0))
        else:
            chain = product(chain_factor[0, i - 1], inverse_all[i])
            panel = -jnp.where(chosen[i], gathered + product(panels[-1], chain), 0.0)
            cross = -(product(panels[-1].T, scaled[i]) + product(blocks[-1], chain))
            block = product(left.T, jnp.concatenate([mine[i], -panel], axis=0)) - product(
                chain.T, cross
            )
            crosses.append(cross)
        panels.append(panel)
        blocks.append(block)
    total = lax.psum(jnp.stack(blocks + crosses), "row")
    return (jnp.stack(panels)[None], total[None])


def solution(mesh):
    in_specs = (
        P("row", "branch"),
        P("branch", None, None, None),
        P("branch", None, "row", None),
        P("branch", None, None, None),
        P("branch", None),
    )
    out_specs = (P("branch", None, "row", None), P("branch", None, None, None))
    return jax.shard_map(
        on_device, mesh=mesh, in_specs=in_specs, out_specs=out_specs, check_vma=False
    )
```

profile of v0, /device:TPU:1, one launch (start us, length us, event | category | flops | bytes accessed | tf_op | source)
XLA Modules:
  0.0 239.7 jit_solution(12061691324562750237)
XLA Ops:
  7.2 0.7 all-gather.3.cloned.1.call-update
  7.9 17.2 %inverses.1 = f32[3,576,576]{2,1,0:T(8,128)S(1)} custom-call(f32[1,3,576,576]{3,2,1,0:T(8,128)} %l_ref.1), custom_call_target="tpu_custom_call" | custom-call | tf_op jit(solution)/shard_map/inverses/pallas_call | solution.py:83
  25.1 2.0 copy-done
  27.2 2.7 %fusion.24 = (bf16[288,576]{1,0:T(8,128)(2,1)S(1)}, f32[288,576]{1,0:T(8,128)S(1)}) fusion(f32[3,576,576]{2,1,0:T(8,128)} %copy-done, f32[1,3,288,576]{3,2,1,0:T(8,128)S(1)} %copy-done.4, pred[]{:T(512)} %bitcast.11), kind=kOutput, calls=%fused_computation.33 | convolution fusion | flops 573640704 | bytes 3207680 | tf_op jit(solution)/shard_map/dot_general | solution.py:15
  29.9 0.1 collective-permute-start
  30.0 0.7 compare_reduce_fusion
  30.7 3.5 %fusion.16 = f32[288,576]{1,0:T(8,128)S(1)} fusion(f32[3,576,576]{2,1,0:T(8,128)} %copy-done, f32[1,3,288,576]{3,2,1,0:T(8,128)S(1)} %copy-done.4, pred[]{:T(512)} %compare_reduce_fusion), kind=kOutput, calls=%fused_computation.17 | convolution fusion | flops 573474816 | bytes 2875904 | tf_op jit(solution)/shard_map/dot_general | solution.py:15
  34.2 0.7 compare_reduce_fusion.1
  34.9 1.9 fusion.17
  36.9 0.1 convert_bitcast_fusion
  37.0 0.1 pad_maximum_fusion.2.x_ref
  37.1 1.5 pad_maximum_fusion.1.scaled_ref
  38.6 1.1 copy-done.3
  39.7 2.2 fusion.10
  42.0 3.3 %fusion.7 = f32[1,576,576]{2,1,0:T(8,128)} fusion(f32[1,2,576,576]{3,2,1,0:T(8,128)S(1)} %copy-done.3, f32[3,576,576]{2,1,0:T(8,128)S(1)} %copy-done.1), kind=kOutput, calls=%fused_computation.12 | convolution fusion | flops 1146617856 | bytes 4276224 | tf_op jit(solution)/shard_map/dot_general | solution.py:15
  45.3 1.4 add_convert_fusion.keep_ref
  46.7 55.5 %line_gather.1.all_ref = bf16[8,2,288,576]{3,2,1,0:T(8,128)(2,1)S(1)} custom-call(bf16[2,288,576]{2,1,0:T(8,128)(2,1)S(1)} %pad_maximum_fusion.2.x_ref), custom_call_target="tpu_custom_call" | custom-call | tf_op jit(solution)/shard_map/line_gather/pallas_call | solution.py:330
  102.2 2.6 %copy-done.2 = bf16[8,2,288,576]{3,2,1,0:T(8,128)(2,1)} copy-done((bf16[8,2,288,576]{3,2,1,0:T(8,128)(2,1)}, bf16[8,2,288,576]{3,2,1,0:T(8,128)(2,1)S(1)}, u32[]{:S(2)}) %copy-start.2) | copy-done | bytes 5308440
  104.8 1.1 constant_dynamic-slice_fusion.mine_ref
  105.9 3.4 %pad_maximum_fusion.chain_ref = f32[2,576,576]{2,1,0:T(8,128)} fusion(f32[1,576,576]{2,1,0:T(8,128)S(1)} %fusion.10, f32[1,576,576]{2,1,0:T(8,128)} %fusion.7), kind=kLoop, calls=%fused_computation | loop fusion | flops 663552 | bytes 5308416 | tf_op jit(solution)/shard_map/stack | solution.py:429
  109.3 0.3 maximum_select_fusion.pair_ref
  109.6 28.9 %partials.1 = (f32[1,3,288,576]{3,2,1,0:T(8,128)}, f32[2944,576]{1,0:T(8,128)}) custom-call(s32[3]{0:T(128)S(1)} %add_convert_fusion.keep_ref, bf16[4,288,576]{2,1,0:T(8,128)(2,1)} %bitcast.67, bf16[8,2,288,576]{3,2,1,0:T(8,128)(2,1)} %copy-done.2, bf16[576,576]{1,0:T(8,128)(2,1)S(1)} %maximum_select_fusion.pair_ref, ...), custom_call_target="tpu_custom_call" | custom-call | tf_op jit(solution)/shard_map/partials/pallas_call | solution.py:385
  138.5 87.7 %line_sum.1 = f32[2,4,368,576]{3,2,1,0:T(8,128)} custom-call(f32[2,4,368,576]{3,2,1,0:T(8,128)} %bitcast.62), custom_call_target="tpu_custom_call" | custom-call | tf_op jit(solution)/shard_map/line_sum/pallas_call | solution.py:224
  226.2 6.6 %slice.49 = f32[2880,576]{1,0:T(8,128)} slice(f32[2944,576]{1,0:T(8,128)} %bitcast.61), slice={[0:2880], [0:576]} | slice | bytes 13271040 | tf_op jit(solution)/shard_map/slice | solution.py:243
  (12 shorter events, 0.1 us)
Async XLA Ops:
  7.2 102.4 %all-gather.3.cloned.1.call-start = ((), (), s32[]{:S(2)}) async-start(), calls=%async_computation | async-start | bytes 1843200 | tf_op jit(solution)/shard_map/all_gather | solution.py:407
  7.9 19.2 %copy-start.5 = (s32[1,3]{1,0:T(1,128)S(1)}, s32[1,3]{1,0:T(1,128)}, u32[]{:S(2)}) copy-start(s32[1,3]{1,0:T(1,128)} %param.9) | copy-start | bytes 40
  7.9 19.3 %copy-start.4 = (f32[1,3,288,576]{3,2,1,0:T(8,128)S(1)}, f32[1,3,288,576]{3,2,1,0:T(8,128)}, u32[]{:S(2)}) copy-start(f32[1,3,288,576]{3,2,1,0:T(8,128)} %param.7) | copy-start | bytes 5971972
  25.1 2.0 copy-start
  27.2 7.7 %copy-start.1 = (f32[3,576,576]{2,1,0:T(8,128)S(1)}, f32[3,576,576]{2,1,0:T(8,128)}, u32[]{:S(2)}) copy-start(f32[3,576,576]{2,1,0:T(8,128)} %copy-done) | copy-start | bytes 11943940
  29.9 79.4 %collective-permute-start = (bf16[288,576]{1,0:T(8,128)(2,1)S(1)}, bf16[288,576]{1,0:T(8,128)(2,1)S(1)}, u32[]{:S(2)}, u32[]{:S(2)}) collective-permute-start(bf16[288,576]{1,0:T(8,128)(2,1)S(1)} %get-tuple-element.6), channel_id=1, source_target_pairs={{0,1},{1,0},{2,3},{3,2},{4,5},{5,4},{6,7},{7,6},{8,9},{9,8},{10,11... | collective-permute-start | bytes 995336 | tf_op jit(solution)/shard_map/ppermute | solution.py:422
  37.1 2.6 %copy-start.3 = (f32[1,2,576,576]{3,2,1,0:T(8,128)S(1)}, f32[1,2,576,576]{3,2,1,0:T(8,128)}, u32[]{:S(2)}) copy-start(f32[1,2,576,576]{3,2,1,0:T(8,128)} %param.8) | copy-start | bytes 7962628
  102.2 2.6 %copy-start.2 = (bf16[8,2,288,576]{3,2,1,0:T(8,128)(2,1)}, bf16[8,2,288,576]{3,2,1,0:T(8,128)(2,1)S(1)}, u32[]{:S(2)}) copy-start(bf16[8,2,288,576]{3,2,1,0:T(8,128)(2,1)S(1)} %line_gather.1.all_ref) | copy-start | bytes 15925252
Sparse Core Ops, SparseCore 0:
  9.8 32.2 all-gather.2
where the time goes:
time: 240 us
  Pallas kernels  189 us (79%)
  between operations  14.2 us (6%)
  matrix products  13.7 us (6%)
  local copies, waits for them, and re-layouts  13.4 us (6%)
  other arithmetic  8.23 us (3%)
    pallas_call x1, Pallas kernels, line_sum(): pl.pallas_call(sum_kernel, out_shape=jax.ShapeDtypeStruct((2, 4, rows, co...  87.7 us
    pallas_call x1, Pallas kernels, line_gather(): pl.pallas_call(gather_kernel, out_shape=jax.ShapeDtypeStruct((8, *x.shape...  55.5 us
    pallas_call x1, Pallas kernels, partials(): pl.pallas_call(functools.partial(partial_kernel, size), out_shape=(jax.Sh...  28.9 us
    pallas_call x1, Pallas kernels, inverses(): pl.pallas_call(functools.partial(inverse_kernel, size, size // 3), grid=(...  17.2 us
    dot_general x5, matrix products, product(): jnp.dot(left_mat, right_mat, precision=lax.Precision.HIGH, preferred_elem...  13.7 us
    slice x1, local copies, waits for them, and re-layouts, line_sum(): return out.reshape(8 * rows, columns)[:total]  6.63 us
    unnamed x12, local copies, waits for them, and re-layouts  5.7 us
  transfers between devices with their start and end apart: 2, of which 0 were waited for; matrix products, arithmetic and copies ran while one was open for 10% of the time, Pallas kernels for 30%

commit v1 on v0

--- a/solution.py
+++ b/solution.py
@@ -166,7 +166,7 @@
     pl.when(goes_right(1))(rights[1].start)
     pl.when(goes_left(1))(lefts[1].start)
     sibs[0].start()
-    out_ref[core, z] = final[...].astype(F32)
+    out_ref[core, z] = pair[0]
     for s in (1, 2, 3):
         @pl.when(z >= s)
         def _():

time: 240 us -> 240 us (level)
  no operation moved by 1% of the time
where the time goes in v1:
time: 240 us
  Pallas kernels  189 us (79%)
  between operations  14.2 us (6%)
  matrix products  13.7 us (6%)
  local copies, waits for them, and re-layouts  13.4 us (6%)
  other arithmetic  8.23 us (3%)
    pallas_call x1, Pallas kernels, line_sum(): pl.pallas_call(sum_kernel, out_shape=jax.ShapeDtypeStruct((2, 4, rows, co...  87.7 us
    pallas_call x1, Pallas kernels, line_gather(): pl.pallas_call(gather_kernel, out_shape=jax.ShapeDtypeStruct((8, *x.shape...  55.5 us
    pallas_call x1, Pallas kernels, partials(): pl.pallas_call(functools.partial(partial_kernel, size), out_shape=(jax.Sh...  28.9 us
    pallas_call x1, Pallas kernels, inverses(): pl.pallas_call(functools.partial(inverse_kernel, size, size // 3), grid=(...  17.2 us
    dot_general x5, matrix products, product(): jnp.dot(left_mat, right_mat, precision=lax.Precision.HIGH, preferred_elem...  13.7 us
    slice x1, local copies, waits for them, and re-layouts, line_sum(): return out.reshape(8 * rows, columns)[:total]  6.63 us
    unnamed x12, local copies, waits for them, and re-layouts  5.7 us
  transfers between devices with their start and end apart: 2, of which 0 were waited for; matrix products, arithmetic and copies ran while one was open for 10% of the time, Pallas kernels for 30%

profile of v1, /device:TPU:1, one launch (start us, length us, event | category | flops | bytes accessed | tf_op | source)
XLA Modules:
  0.0 239.7 jit_solution(14181713455368546303)
XLA Ops:
  7.2 0.7 all-gather.3.cloned.1.call-update
  7.9 17.2 %inverses.1 = f32[3,576,576]{2,1,0:T(8,128)S(1)} custom-call(f32[1,3,576,576]{3,2,1,0:T(8,128)} %l_ref.1), custom_call_target="tpu_custom_call" | custom-call | tf_op jit(solution)/shard_map/inverses/pallas_call | solution.py:83
  25.1 2.0 copy-done
  27.2 2.7 %fusion.24 = (bf16[288,576]{1,0:T(8,128)(2,1)S(1)}, f32[288,576]{1,0:T(8,128)S(1)}) fusion(f32[3,576,576]{2,1,0:T(8,128)} %copy-done, f32[1,3,288,576]{3,2,1,0:T(8,128)S(1)} %copy-done.4, pred[]{:T(512)} %bitcast.11), kind=kOutput, calls=%fused_computation.33 | convolution fusion | flops 573640704 | bytes 3207680 | tf_op jit(solution)/shard_map/dot_general | solution.py:15
  29.9 0.1 collective-permute-start
  30.0 0.7 compare_reduce_fusion
  30.7 3.5 %fusion.16 = f32[288,576]{1,0:T(8,128)S(1)} fusion(f32[3,576,576]{2,1,0:T(8,128)} %copy-done, f32[1,3,288,576]{3,2,1,0:T(8,128)S(1)} %copy-done.4, pred[]{:T(512)} %compare_reduce_fusion), kind=kOutput, calls=%fused_computation.17 | convolution fusion | flops 573474816 | bytes 2875904 | tf_op jit(solution)/shard_map/dot_general | solution.py:15
  34.2 0.7 compare_reduce_fusion.1
  34.9 1.9 fusion.17
  36.9 0.1 convert_bitcast_fusion
  37.0 0.1 pad_maximum_fusion.2.x_ref
  37.1 1.5 pad_maximum_fusion.1.scaled_ref
  38.6 1.1 copy-done.3
  39.7 2.2 fusion.10
  42.0 3.3 %fusion.7 = f32[1,576,576]{2,1,0:T(8,128)} fusion(f32[1,2,576,576]{3,2,1,0:T(8,128)S(1)} %copy-done.3, f32[3,576,576]{2,1,0:T(8,128)S(1)} %copy-done.1), kind=kOutput, calls=%fused_computation.12 | convolution fusion | flops 1146617856 | bytes 4276224 | tf_op jit(solution)/shard_map/dot_general | solution.py:15
  45.3 1.4 add_convert_fusion.keep_ref
  46.7 55.5 %line_gather.1.all_ref = bf16[8,2,288,576]{3,2,1,0:T(8,128)(2,1)S(1)} custom-call(bf16[2,288,576]{2,1,0:T(8,128)(2,1)S(1)} %pad_maximum_fusion.2.x_ref), custom_call_target="tpu_custom_call" | custom-call | tf_op jit(solution)/shard_map/line_gather/pallas_call | solution.py:330
  102.2 2.6 %copy-done.2 = bf16[8,2,288,576]{3,2,1,0:T(8,128)(2,1)} copy-done((bf16[8,2,288,576]{3,2,1,0:T(8,128)(2,1)}, bf16[8,2,288,576]{3,2,1,0:T(8,128)(2,1)S(1)}, u32[]{:S(2)}) %copy-start.2) | copy-done | bytes 5308440
  104.8 1.1 constant_dynamic-slice_fusion.mine_ref
  105.9 3.4 %pad_maximum_fusion.chain_ref = f32[2,576,576]{2,1,0:T(8,128)} fusion(f32[1,576,576]{2,1,0:T(8,128)S(1)} %fusion.10, f32[1,576,576]{2,1,0:T(8,128)} %fusion.7), kind=kLoop, calls=%fused_computation | loop fusion | flops 663552 | bytes 5308416 | tf_op jit(solution)/shard_map/stack | solution.py:429
  109.3 0.3 maximum_select_fusion.pair_ref
  109.6 28.9 %partials.1 = (f32[1,3,288,576]{3,2,1,0:T(8,128)}, f32[2944,576]{1,0:T(8,128)}) custom-call(s32[3]{0:T(128)S(1)} %add_convert_fusion.keep_ref, bf16[4,288,576]{2,1,0:T(8,128)(2,1)} %bitcast.67, bf16[8,2,288,576]{3,2,1,0:T(8,128)(2,1)} %copy-done.2, bf16[576,576]{1,0:T(8,128)(2,1)S(1)} %maximum_select_fusion.pair_ref, ...), custom_call_target="tpu_custom_call" | custom-call | tf_op jit(solution)/shard_map/partials/pallas_call | solution.py:385
  138.5 87.7 %line_sum.1 = f32[2,4,368,576]{3,2,1,0:T(8,128)} custom-call(f32[2,4,368,576]{3,2,1,0:T(8,128)} %bitcast.62), custom_call_target="tpu_custom_call" | custom-call | tf_op jit(solution)/shard_map/line_sum/pallas_call | solution.py:224
  226.2 6.6 %slice.49 = f32[2880,576]{1,0:T(8,128)} slice(f32[2944,576]{1,0:T(8,128)} %bitcast.61), slice={[0:2880], [0:576]} | slice | bytes 13271040 | tf_op jit(solution)/shard_map/slice | solution.py:243
  (12 shorter events, 0.1 us)
Async XLA Ops:
  7.2 102.4 %all-gather.3.cloned.1.call-start = ((), (), s32[]{:S(2)}) async-start(), calls=%async_computation | async-start | bytes 1843200 | tf_op jit(solution)/shard_map/all_gather | solution.py:407
  7.9 19.2 %copy-start.5 = (s32[1,3]{1,0:T(1,128)S(1)}, s32[1,3]{1,0:T(1,128)}, u32[]{:S(2)}) copy-start(s32[1,3]{1,0:T(1,128)} %param.9) | copy-start | bytes 40
  7.9 19.3 %copy-start.4 = (f32[1,3,288,576]{3,2,1,0:T(8,128)S(1)}, f32[1,3,288,576]{3,2,1,0:T(8,128)}, u32[]{:S(2)}) copy-start(f32[1,3,288,576]{3,2,1,0:T(8,128)} %param.7) | copy-start | bytes 5971972
  25.1 2.0 copy-start
  27.2 7.7 %copy-start.1 = (f32[3,576,576]{2,1,0:T(8,128)S(1)}, f32[3,576,576]{2,1,0:T(8,128)}, u32[]{:S(2)}) copy-start(f32[3,576,576]{2,1,0:T(8,128)} %copy-done) | copy-start | bytes 11943940
  29.9 79.4 %collective-permute-start = (bf16[288,576]{1,0:T(8,128)(2,1)S(1)}, bf16[288,576]{1,0:T(8,128)(2,1)S(1)}, u32[]{:S(2)}, u32[]{:S(2)}) collective-permute-start(bf16[288,576]{1,0:T(8,128)(2,1)S(1)} %get-tuple-element.6), channel_id=1, source_target_pairs={{0,1},{1,0},{2,3},{3,2},{4,5},{5,4},{6,7},{7,6},{8,9},{9,8},{10,11... | collective-permute-start | bytes 995336 | tf_op jit(solution)/shard_map/ppermute | solution.py:422
  37.1 2.6 %copy-start.3 = (f32[1,2,576,576]{3,2,1,0:T(8,128)S(1)}, f32[1,2,576,576]{3,2,1,0:T(8,128)}, u32[]{:S(2)}) copy-start(f32[1,2,576,576]{3,2,1,0:T(8,128)} %param.8) | copy-start | bytes 7962628
  102.2 2.6 %copy-start.2 = (bf16[8,2,288,576]{3,2,1,0:T(8,128)(2,1)}, bf16[8,2,288,576]{3,2,1,0:T(8,128)(2,1)S(1)}, u32[]{:S(2)}) copy-start(bf16[8,2,288,576]{3,2,1,0:T(8,128)(2,1)S(1)} %line_gather.1.all_ref) | copy-start | bytes 15925252
Sparse Core Ops, SparseCore 0:
  9.8 32.2 all-gather.2
